TPU v7x, 512 devices: a whole 4x4x16 slice. The times are simulated.
512 devices in a mesh: expert: 64 (over z, y_lo, core), tensor: 8 (over y_hi, x).
Axes of the slice: x: 4, y: 4 (y_hi: 2, y_lo: 2; y = y_hi * 2 + y_lo), z: 16, core: 2. Of those that a mesh axis runs over, the one named last changes fastest.
Arguments:
- tokens: bfloat16 [16384, 2048], P('expert', 'tensor'), may hold values from -6 to 6
- gate_values: float32 [16384, 2], P('expert'), may hold values from 0.25 to 1
- expert_ids: int32 [16384, 2], P('expert'), may hold values from 0 to 63, as said below
- slot_index: int32 [16384, 2], P('expert'), may hold values from -1 to 9, as said below
- w_in: bfloat16 [64, 2048, 4096], P('expert', None, 'tensor'), may hold values from -0.125 to 0.125
- w_out: bfloat16 [64, 4096, 2048], P('expert', 'tensor'), may hold values from -0.09375 to 0.09375
Outputs:
- combined: bfloat16 [16384, 2048], P('expert', 'tensor')
Inputs may be any that keep to these rules, and one draw needn't show every extreme that they name: `expert_ids`: the 2 experts of a token differ. `slot_index`: within each source block of 256 tokens, with choices taken in order of token and then of choice, the i-th choice of an expert (i from 0) has slot i if i < 10 and -1 otherwise.
All inputs are finite; a program needn't handle non-finite values.
Results may differ from a plain program's by a relative error of at most 0.019.
Values may be sent and summed in bfloat16 or wider, within the bound.
A program may use at most 64 MiB of HBM per device.

v0:
```python
import jax
import jax.numpy as jnp
from jax import lax
from jax.sharding import PartitionSpec as P


def body(tokens, gate_values, expert_ids, slot_index, w_in, w_out):
    experts = lax.axis_size("expert") * w_in.shape[0]
    tok_rows = tokens.shape[0]
    capacity = 5 * tok_rows * expert_ids.shape[1] // (4 * experts)
    panel_rows = experts * capacity
    is_kept = slot_index >= 0
    target = jnp.where(is_kept, expert_ids * capacity + slot_index, -1)
    rows_iota = lax.broadcasted_iota(jnp.int32, (panel_rows, tok_rows), 0)
    dispatch = (target[:, 0][None, :] == rows_iota).astype(jnp.bfloat16) + (
        target[:, 1][None, :] == rows_iota
    ).astype(jnp.bfloat16)
    in_weight = w_in[0]
    out_weight = w_out[0]
    panel_data = jnp.dot(
        dispatch,
        lax.all_gather(tokens, "tensor", axis=1, tiled=True),
        preferred_element_type=jnp.float32,
    ).astype(jnp.bfloat16)
    arrived = lax.all_to_all(
        panel_data.reshape(experts, capacity, -1), "expert", split_axis=0, concat_axis=0, tiled=True
    )
    hidden_pre = jnp.dot(
        arrived.reshape(panel_rows, -1), in_weight, preferred_element_type=jnp.float32
    )
    hidden = jax.nn.gelu(hidden_pre, approximate=True).astype(jnp.bfloat16)
    partial_value = jnp.dot(hidden, out_weight, preferred_element_type=jnp.float32)
    summed = lax.psum_scatter(
        partial_value.astype(jnp.bfloat16), "tensor", scatter_dimension=1, tiled=True
    )
    returned = lax.all_to_all(
        summed.reshape(experts, capacity, -1), "expert", split_axis=0, concat_axis=0, tiled=True
    )
    returned = returned.reshape(panel_rows, -1)
    safe_rows = jnp.where(is_kept, target, 0)
    weight = jnp.where(is_kept, gate_values, 0.0)
    first_pick = jnp.take(returned, safe_rows[:, 0], axis=0).astype(jnp.float32)
    second_pick = jnp.take(returned, safe_rows[:, 1], axis=0).astype(jnp.float32)
    combined = weight[:, 0:1] * first_pick + weight[:, 1:2] * second_pick
    return combined.astype(jnp.bfloat16)


def solution(mesh):
    placed = (
        P("expert", "tensor"),
        P("expert", None),
        P("expert", None),
        P("expert", None),
        P("expert", None, "tensor"),
        P("expert", "tensor", None),
    )
    return jax.shard_map(
        body, mesh=mesh, in_specs=placed, out_specs=P("expert", "tensor"), check_vma=False
    )
```

profile of v0, /device:TPU:1, one launch (start us, length us, event | category | flops | bytes accessed | tf_op | source)
XLA Modules:
  0.0 446.4 jit_solution(12879730159829166891)
XLA Ops:
  6.5 0.0 copy-start
  6.5 0.0 all-gather.2.cloned.1.call-start
  6.5 0.7 all-gather.2.cloned.1.call-update
  7.3 0.0 reduce-scatter.2.cloned.1.call-start
  7.3 0.7 broadcast_select_fusion.1
  8.0 69.9 %all-gather.2.cloned.1.call-done = bf16[256,2048]{1,0:T(8,128)(2,1)} async-done(((bf16[256,256]{1,0:T(8,128)(2,1)}), bf16[256,2048]{1,0:T(8,128)(2,1)}) %all-gather.2.cloned.1.call-update) | async-done | bytes 1048592 | tf_op jit(solution)/shard_map/all_gather | solution.py:22
  77.9 3.6 convolution_convert_fusion.1
  81.6 5.3 %reshape.19 = bf16[64,10,2048]{2,1,0:T(8,128)(2,1)} reshape(bf16[640,2048]{1,0:T(8,128)(2,1)} %convolution_convert_fusion.1) | data formatting | bytes 5242880 | tf_op jit(solution)/shard_map/reshape | solution.py:26
  86.9 203.1 %all_to_all.10 = bf16[64,10,2048]{2,1,0:T(8,128)(2,1)} all-to-all(bf16[64,10,2048]{2,1,0:T(8,128)(2,1)} %reshape.19), channel_id=1, replica_groups=mesh['expert'=64,'tensor'=8] {'expert'}, dimensions={0} | all-to-all | bytes 5242880 | tf_op jit(solution)/shard_map/all_to_all | solution.py:25
  290.0 5.5 %reshape.20 = bf16[640,2048]{1,0:T(8,128)(2,1)} reshape(bf16[64,10,2048]{2,1,0:T(8,128)(2,1)} %all_to_all.10) | data formatting | bytes 5242880 | tf_op jit(solution)/shard_map/reshape | solution.py:29
  295.6 0.0 copy-done
  295.6 7.0 %convolution_convert_fusion = bf16[640,2048]{1,0:T(8,128)(2,1)} fusion(bf16[1,512,2048]{2,1,0:T(8,128)(2,1)S(1)} %copy-done, bf16[640,2048]{1,0:T(8,128)(2,1)} %reshape.20, bf16[1,2048,512]{2,1,0:T(8,128)(2,1)} %param.12), kind=kOutput, calls=%fused_computation.2 | convolution fusion | flops 2688614400 | bytes 9437184 | tf_op jit(solution)/shard_map/dot_general | solution.py:32
  302.6 0.0 copy-start.1
  302.6 0.0 copy-start.2
  302.6 0.0 reduce-scatter.2.cloned.1.call-update
  302.6 84.5 %reduce-scatter.2.cloned.1.call-done = bf16[640,256]{1,0:T(8,128)(2,1)} async-done(((bf16[640,2048]{1,0:T(8,128)(2,1)}), bf16[640,256]{1,0:T(8,128)(2,1)}) %reduce-scatter.2.cloned.1.call-update) | async-done | bytes 327696 | tf_op jit(solution)/shard_map/reduce_scatter | solution.py:33
  387.1 1.9 reshape.21
  389.0 14.8 %all-to-all-start.1 = ((bf16[64,10,256]{2,1,0:T(8,128)(2,1)}), bf16[64,10,256]{2,1,0:T(8,128)(2,1)S(1)}, u32[]{:S(2)}, u32[]{:S(2)}) async-start(bf16[64,10,256]{2,1,0:T(8,128)(2,1)} %reshape.21), calls=%async_computation.2 | async-start | bytes 1048576 | tf_op jit(solution)/shard_map/all_to_all | solution.py:36
  403.8 0.0 copy-done.1
  403.8 0.0 copy-done.2
  403.8 32.4 %all-to-all-done.1 = bf16[64,10,256]{2,1,0:T(8,128)(2,1)S(1)} async-done(((bf16[64,10,256]{2,1,0:T(8,128)(2,1)}), bf16[64,10,256]{2,1,0:T(8,128)(2,1)S(1)}, u32[]{:S(2)}, u32[]{:S(2)}) %all-to-all-start.1) | async-done | bytes 327712 | tf_op jit(solution)/shard_map/all_to_all | solution.py:36
  436.3 0.1 reshape.22
  436.4 1.2 gather_fusion
  437.5 1.2 gather_fusion.1
  438.7 0.9 add_convert_fusion
  (9 shorter events, 0.1 us)
Async XLA Ops:
  6.5 289.0 %copy-start = (bf16[1,512,2048]{2,1,0:T(8,128)(2,1)S(1)}, bf16[1,512,2048]{2,1,0:T(8,128)(2,1)}, u32[]{:S(2)}) copy-start(bf16[1,512,2048]{2,1,0:T(8,128)(2,1)} %param.13) | copy-start | bytes 6291460
  6.5 71.4 %all-gather.2.cloned.1.call-start = ((), (), s32[]{:S(2)}) async-start(), calls=%async_computation.3 | async-start | bytes 1179648 | tf_op jit(solution)/shard_map/all_gather | solution.py:22
  7.3 379.8 %reduce-scatter.2.cloned.1.call-start = ((), (), s32[]{:S(2)}) async-start(), calls=%async_computation.4 | async-start | bytes 2949120 | tf_op jit(solution)/shard_map/reduce_scatter | solution.py:33
  302.6 101.2 %copy-start.1 = (s32[256,2]{0,1:T(2,128)S(1)}, s32[256,2]{0,1:T(2,128)}, u32[]{:S(2)}) copy-start(s32[256,2]{0,1:T(2,128)} %param.11) | copy-start | bytes 6148
  302.6 101.2 %copy-start.2 = (f32[256,2]{0,1:T(2,128)S(1)}, f32[256,2]{0,1:T(2,128)}, u32[]{:S(2)}) copy-start(f32[256,2]{0,1:T(2,128)} %param.9) | copy-start | bytes 6148
  389.0 47.3 %all-to-all-start.1 = ((bf16[64,10,256]{2,1,0:T(8,128)(2,1)}), bf16[64,10,256]{2,1,0:T(8,128)(2,1)S(1)}, u32[]{:S(2)}, u32[]{:S(2)}) async-start(bf16[64,10,256]{2,1,0:T(8,128)(2,1)} %reshape.21), calls=%async_computation.2 | async-start | bytes 1048576 | tf_op jit(solution)/shard_map/all_to_all | solution.py:36
Sparse Core Ops, SparseCore 0:
  10.4 67.4 all-gather.1
  302.7 84.3 reduce-scatter.1
where the time goes:
time: 447 us; the launch traced here: 446 us
  blocking collectives  203 us (45%)
  waiting for transfers between devices  188 us (42%)
  local copies, waits for them, and re-layouts  15.2 us (3%)
  starting transfers between devices  14.8 us (3%)
  between operations  13.5 us (3%)
  matrix products  10.6 us (2%)
    all_to_all x1, blocking collectives, body(): lax.all_to_all(panel_data.reshape(experts, capacity, -1), 'expert', split...  203 us
    reduce_scatter x1, waiting for transfers between devices, body(): lax.psum_scatter(partial_value.astype(jnp.bfloat16), 'tensor', scatter_di...  84.5 us
    all_gather x1, waiting for transfers between devices, body(): lax.all_gather(tokens, 'tensor', axis=1, tiled=True)  69.9 us
    all_to_all x1, waiting for transfers between devices, body(): lax.all_to_all(summed.reshape(experts, capacity, -1), 'expert', split_axi...  32.4 us
    all_to_all x1, starting transfers between devices, body(): lax.all_to_all(summed.reshape(experts, capacity, -1), 'expert', split_axi...  14.8 us
  transfers between devices with their start and end apart: 3, of which 3 were waited for; matrix products, arithmetic and copies ran while one was open for 0% of the time, Pallas kernels for 0%

commit v1 on v0

v1 whole, which is shorter than its diff:
```python
import functools

import jax
import jax.numpy as jnp
from jax import lax
from jax.experimental import pallas as pl
from jax.experimental.pallas import tpu as pltpu
from jax.sharding import PartitionSpec as P

MESH = pl.DeviceIdType.MESH
BF, F32 = jnp.bfloat16, jnp.float32

NZ = 16
SUB = 4
CAP = 10
PEERS = 8
UNIT = SUB * CAP
DZ = (0, 2, 1, -2, -1, 4, 3, -4, -3, 6, 5, -6, -5, 7, 8, -7)
SLOT_OF = {d % NZ: k for k, d in enumerate(DZ)}
BACK = tuple(SLOT_OF[(-d) % NZ] for d in DZ)
GROUPS = 4
PER = NZ // GROUPS
OFFS = tuple((h, x) for h in range(2) for x in range(4))
OFF_BACK = tuple(OFFS.index((h, (-x) % 4)) for h, x in OFFS)


def places():
    e, t = lax.axis_index("expert"), lax.axis_index("tensor")
    return e // 4, (e // 2) % 2, e % 2, t // 4, t % 4


def kernel(tok, ids, slot, gate, w_in, w_out, out,
           w1, w2, mix, unmix, gates_hi, gates_lo,
           near_out, near_in, far_out, far_in, part_out, part_in,
           back_out, back_in, last_out, last_in,
           w_sem, near_s, near_r, far_s, far_r, ag_s, ag_r, rs_s, rs_r,
           back_s, back_r, last_s, last_r):
    z, ylo, core, yhi, x = places()
    tens = yhi * 4 + x

    def at_sub(i):
        return (z * 4 + ((ylo + i // 2) % 2) * 2 + (core + i % 2) % 2, tens)

    def at_z(d):
        return (((z + d + NZ) % NZ) * 4 + ylo * 2 + core, tens)

    def peer_index(r):
        h, dx = OFFS[r]
        return ((yhi + h) % 2) * 4 + (x + dx) % 4

    def at_peer(r):
        return (z * 4 + ylo * 2 + core, peer_index(r))

    def remote(src, dst, s, r, to):
        return pltpu.make_async_remote_copy(
            src_ref=src, dst_ref=dst, send_sem=s, recv_sem=r,
            device_id=to, device_id_type=MESH)

    barrier = pltpu.get_barrier_semaphore()
    partners = ([at_sub(i) for i in range(1, SUB)] + [at_z(d) for d in DZ[1:]]
                + [at_peer(r) for r in range(1, PEERS)])
    for p in partners:
        pl.semaphore_signal(barrier, inc=1, device_id=p, device_id_type=MESH)

    loads = []
    for r in range(PEERS):
        j = peer_index(r)
        for h in range(2):
            loads.append(pltpu.make_async_copy(
                w_in.at[0, pl.ds(pl.multiple_of(j * 256 + h * 128, 128), 128), :],
                w1.at[h, pl.ds(r * 128, 128), :], w_sem.at[len(loads)]))
        loads.append(pltpu.make_async_copy(
            w_out.at[0, :, pl.ds(pl.multiple_of(j * 256, 256), 256)],
            w2.at[r], w_sem.at[len(loads)]))
    for c in loads:
        c.start()

    e = ids[...]
    dz = (e // 4 - z + NZ) % NZ
    k = jnp.zeros_like(e)
    for d, s in SLOT_OF.items():
        k = jnp.where(dz == d, s, k)
    sub = ((e // 2 % 2 + ylo) % 2) * 2 + (e % 2 + core) % 2
    c = slot[...]
    target = jnp.where(c >= 0, sub * (NZ * CAP) + k * CAP + c, -1)
    rows = lax.broadcasted_iota(jnp.int32, (SUB * NZ * CAP, 256), 0)
    hit0, hit1 = rows == target[0:1, :], rows == target[1:2, :]
    panel = jnp.dot((hit0 | hit1).astype(F32).astype(BF), tok[...], preferred_element_type=F32)
    near_out[...] = panel.astype(BF).reshape(SUB, NZ * CAP, 256)

    pl.semaphore_wait(barrier, len(partners))

    near = []
    for i in range(1, SUB):
        cp = remote(near_out.at[i], near_in.at[i], near_s.at[i], near_r.at[i], at_sub(i))
        cp.start()
        near.append(cp)
    near_in[0] = near_out[0]

    def near_of_far(i, swap):
        kk = (i * 1639) >> 16
        if swap:
            kk = kk + 1 - 2 * (kk % 2)
        rest = i - ((i * 1639) >> 16) * 40
        ss = (rest * 205) >> 11
        return ss * (NZ * CAP) + kk * CAP + rest - ss * 10

    n = SUB * NZ * CAP
    col_i = lax.broadcasted_iota(jnp.int32, (n, n), 1)
    row_i = lax.broadcasted_iota(jnp.int32, (n, n), 0)
    far_rows = lax.broadcasted_iota(jnp.int32, (n, 1), 0)
    far_cols = lax.broadcasted_iota(jnp.int32, (1, n), 1)
    for h in range(2):
        mix[h] = (near_of_far(far_rows, h) == col_i).astype(F32).astype(BF)
        unmix[h] = (near_of_far(far_cols, h) == row_i).astype(F32).astype(BF)

    g = gate[...]
    weighted = jnp.where(hit0, g[0:1, :], 0.0) + jnp.where(hit1, g[1:2, :], 0.0)
    hi = weighted.astype(BF)
    gates_hi[...] = hi.astype(F32).T.astype(BF)
    gates_lo[...] = (weighted - hi.astype(F32)).T.astype(BF)

    upper = lax.broadcasted_iota(jnp.int32, (2 * UNIT, 128), 0) < UNIT

    def pick(a, b):
        return jnp.where(upper, a, b)

    for cp in near:
        cp.wait_recv()

    arrived = near_in[...].reshape(n, 256)
    order0 = jnp.dot(mix[0], arrived[:, :128], preferred_element_type=F32)
    order1 = jnp.dot(mix[1], arrived[:, 128:], preferred_element_type=F32)
    far = []
    for s in range(NZ):
        a = order0[(s // 2) * 80:(s // 2 + 1) * 80]
        b = order1[(s // 2) * 80:(s // 2 + 1) * 80]
        block = (pick(a, b) if s % 2 == 0 else pick(b, a)).astype(BF)
        if s == 0:
            far_in[0, 0] = block
            continue
        far_out[s] = block
        cp = remote(far_out.at[s], far_in.at[0, BACK[s]], far_s.at[s], far_r.at[BACK[s]],
                    at_z(DZ[s]))
        cp.start()
        far.append(cp)

    gathers, scatters, backs = [], [], []

    def gather(g):
        here = pl.ds(g * PER, PER)
        for s in range(g * PER, (g + 1) * PER):
            if s:
                remote(far_out.at[s], far_in.at[0, s], far_s.at[s], far_r.at[s], at_z(DZ[s])).wait_recv()
        for r in range(1, PEERS):
            cp = remote(far_in.at[0, here], far_in.at[OFF_BACK[r], here],
                        ag_s.at[r, g], ag_r.at[OFF_BACK[r], g], at_peer(r))
            cp.start()
            gathers.append(cp)

    def compute(g):
        here = pl.ds(g * PER, PER)
        for r in range(1, PEERS):
            remote(far_in.at[0, here], far_in.at[r, here],
                   ag_s.at[r, g], ag_r.at[r, g], at_peer(r)).wait_recv()
        left0, left1 = [], []
        for q in range(PER // 2):
            s = g * PER + 2 * q
            a0 = [far_in[r, s] for r in range(PEERS)]
            a1 = [far_in[r, s + 1] for r in range(PEERS)]
            left0.append(jnp.concatenate([pick(u, v) for u, v in zip(a0, a1)], axis=1))
            left1.append(jnp.concatenate([pick(v, u) for u, v in zip(a0, a1)], axis=1))
        acc0 = jnp.dot(jnp.concatenate(left0, axis=0), w1[0], preferred_element_type=F32)
        acc1 = jnp.dot(jnp.concatenate(left1, axis=0), w1[1], preferred_element_type=F32)
        swapped = []
        for q in range(PER // 2):
            swapped += [acc1[q * 80 + 40:q * 80 + 80], acc1[q * 80:q * 80 + 40]]
        v = acc0 + jnp.concatenate(swapped, axis=0)
        inner = 0.7978845608028654 * (v + 0.044715 * (v * v * v))
        hidden = (0.5 * v * (1.0 + jnp.tanh(inner))).astype(BF)
        for r in list(range(1, PEERS)) + [0]:
            res = jnp.dot(hidden, w2[r], preferred_element_type=F32)
            for q in range(PER // 2):
                p0 = res[q * 80:q * 80 + 80, :128]
                p1 = res[q * 80:q * 80 + 80, 128:]
                p1 = jnp.concatenate([p1[40:], p1[:40]], axis=0)
                s = g * PER + 2 * q
                part_out[r, s] = pick(p0, p1).astype(BF)
                part_out[r, s + 1] = pick(p1, p0).astype(BF)
            if r:
                cp = remote(part_out.at[r, here], part_in.at[OFF_BACK[r], here],
                            rs_s.at[r, g], rs_r.at[OFF_BACK[r], g], at_peer(r))
                cp.start()
                scatters.append(cp)

    def finish(g):
        here = pl.ds(g * PER, PER)
        for r in range(1, PEERS):
            remote(part_out.at[r, here], part_in.at[r, here],
                   rs_s.at[r, g], rs_r.at[r, g], at_peer(r)).wait_recv()
        for s in range(g * PER, (g + 1) * PER):
            total = part_out[0, s].astype(F32)
            for r in range(1, PEERS):
                total = total + part_in[r, s].astype(F32)
            if s == 0:
                back_in[0] = total.astype(BF)
                continue
            back_out[s] = total.astype(BF)
            cp = remote(back_out.at[s], back_in.at[BACK[s]], back_s.at[s], back_r.at[BACK[s]],
                        at_z(DZ[s]))
            cp.start()
            backs.append(cp)

    gather(0)
    gather(1)
    for cp in loads:
        cp.wait()
    compute(0)
    gather(2)
    compute(1)
    gather(3)
    finish(0)
    compute(2)
    finish(1)
    compute(3)
    finish(2)
    finish(3)

    for s in range(1, NZ):
        remote(back_out.at[s], back_in.at[s], back_s.at[s], back_r.at[s], at_z(DZ[s])).wait_recv()
    left0, left1 = [], []
    for q in range(NZ // 2):
        a, b = back_in[2 * q], back_in[2 * q + 1]
        left0.append(pick(a, b))
        left1.append(pick(b, a))
    res0 = jnp.dot(unmix[0], jnp.concatenate(left0, axis=0), preferred_element_type=F32)
    res1 = jnp.dot(unmix[1], jnp.concatenate(left1, axis=0), preferred_element_type=F32)
    res = jnp.concatenate([res0, res1], axis=1).astype(BF).reshape(SUB, NZ * CAP, 256)
    last = []
    last_out[...] = res
    for i in range(1, SUB):
        cp = remote(last_out.at[i], last_in.at[i], last_s.at[i], last_r.at[i], at_sub(i))
        cp.start()
        last.append(cp)
    last_in[0] = last_out[0]
    for cp in last:
        cp.wait_recv()
    rows_in = last_in[...].reshape(n, 256)
    out[...] = (jnp.dot(gates_hi[...], rows_in, preferred_element_type=F32)
                + jnp.dot(gates_lo[...], rows_in, preferred_element_type=F32)).astype(BF)
    for cp in near + far + gathers + scatters + backs + last:
        cp.wait_send()


def body(tokens, gate_values, expert_ids, slot_index, w_in, w_out):
    n = SUB * NZ * CAP
    vm = pl.BlockSpec(memory_space=pltpu.VMEM)
    hbm = pl.BlockSpec(memory_space=pl.ANY)
    dma = pltpu.SemaphoreType.DMA
    blocks = (NZ, 2 * UNIT, 128)
    return pl.pallas_call(
        kernel,
        out_shape=jax.ShapeDtypeStruct((256, 256), BF),
        in_specs=[vm, vm, vm, vm, hbm, hbm],
        out_specs=vm,
        scratch_shapes=[
            pltpu.VMEM((2, 1024, 512), BF), pltpu.VMEM((PEERS, 512, 256), BF),
            pltpu.VMEM((2, n, n), BF), pltpu.VMEM((2, n, n), BF),
            pltpu.VMEM((256, n), BF), pltpu.VMEM((256, n), BF),
            pltpu.VMEM((SUB, NZ * CAP, 256), BF), pltpu.VMEM((SUB, NZ * CAP, 256), BF),
            pltpu.VMEM(blocks, BF), pltpu.VMEM((PEERS,) + blocks, BF),
            pltpu.VMEM((PEERS,) + blocks, BF), pltpu.VMEM((PEERS,) + blocks, BF),
            pltpu.VMEM(blocks, BF), pltpu.VMEM(blocks, BF),
            pltpu.VMEM((SUB, NZ * CAP, 256), BF), pltpu.VMEM((SUB, NZ * CAP, 256), BF),
            dma((3 * PEERS,)), dma((SUB,)), dma((SUB,)), dma((NZ,)), dma((NZ,)),
            dma((PEERS, GROUPS)), dma((PEERS, GROUPS)), dma((PEERS, GROUPS)), dma((PEERS, GROUPS)),
            dma((NZ,)), dma((NZ,)), dma((SUB,)), dma((SUB,)),
        ],
        compiler_params=pltpu.CompilerParams(
            collective_id=0, has_side_effects=True, vmem_limit_bytes=48 * 2**20),
        name="moe",
    )(tokens, expert_ids.T, slot_index.T, gate_values.T, w_in, w_out)


def solution(mesh):
    placed = (
        P("expert", "tensor"),
        P("expert", None),
        P("expert", None),
        P("expert", None),
        P("expert", None, "tensor"),
        P("expert", "tensor", None),
    )
    return jax.shard_map(
        body, mesh=mesh, in_specs=placed, out_specs=P("expert", "tensor"), check_vma=False
    )
```

time: 447 us -> 113 us (0.25)
  blocking collectives: 203 us -> 0 us
  waiting for transfers between devices: 188 us -> 0 us
  Pallas kernels: 0 us -> 104 us
  starting transfers between devices: 14.8 us -> 0 us
  between operations: 13.5 us -> 0.02 us
  matrix products: 10.6 us -> 0 us
  local copies, waits for them, and re-layouts: 15.2 us -> 6.79 us
    all_to_all x1 -> x0, blocking collectives: 203 us -> none  [body(): lax.all_to_all(panel_data.reshape(experts, capacity, -1), 'expert', split...]
    pallas_call x0 -> x1, Pallas kernels: none -> 104 us  [body(): pl.pallas_call(kernel, out_shape=jax.ShapeDtypeStruct((256, 256), BF), in...]
    reduce_scatter x1 -> x0, waiting for transfers between devices: 84.5 us -> none  [body(): lax.psum_scatter(partial_value.astype(jnp.bfloat16), 'tensor', scatter_di...]
    all_gather x1 -> x0, waiting for transfers between devices: 69.9 us -> none  [body(): lax.all_gather(tokens, 'tensor', axis=1, tiled=True)]
    all_to_all x1 -> x0, waiting for transfers between devices: 32.4 us -> none  [body(): lax.all_to_all(summed.reshape(experts, capacity, -1), 'expert', split_axi...]
    all_to_all x1 -> x0, starting transfers between devices: 14.8 us -> none  [body(): lax.all_to_all(summed.reshape(experts, capacity, -1), 'expert', split_axi...]
    reshape x4 -> x0, local copies, waits for them, and re-layouts: 12.8 us -> none  [the longest x1 5.53 us: body(): arrived.reshape(panel_rows, -1)]
    dot_general x2 -> x0, matrix products: 10.6 us -> none  [the longest x1 7.01 us: body(): jnp.dot(hidden, out_weight, preferred_element_type=jnp.float32)]
  transfers between devices with their start and end apart: 3 -> 0, of which waited for: 3 -> 0; matrix products, arithmetic and copies ran while one was open for 0% -> 0% of each run, Pallas kernels for 0% -> 0%
where the time goes in v1:
time: 113 us; the launch traced here: 111 us
  Pallas kernels  104 us (92%)
  local copies, waits for them, and re-layouts  6.79 us (6%)
    pallas_call x1, Pallas kernels, body(): pl.pallas_call(kernel, out_shape=jax.ShapeDtypeStruct((256, 256), BF), in...  104 us
    unnamed x13, local copies, waits for them, and re-layouts  6.79 us

profile of v1, /device:TPU:1, one launch (start us, length us, event | category | flops | bytes accessed | tf_op | source)
XLA Modules:
  0.0 111.2 jit_solution(8327335966757554781)
XLA Ops:
  0.0 0.0 copy-start
  0.0 1.6 %copy-done = bf16[1,2048,512]{2,1,0:T(8,128)(2,1)S(1)} copy-done((bf16[1,2048,512]{2,1,0:T(8,128)(2,1)S(1)}, bf16[1,2048,512]{2,1,0:T(8,128)(2,1)}, u32[]{:S(2)}) %copy-start) | copy-done | bytes 2097176
  1.6 0.0 copy-start.1
  1.6 1.6 %copy-done.1 = bf16[1,512,2048]{2,1,0:T(8,128)(2,1)S(1)} copy-done((bf16[1,512,2048]{2,1,0:T(8,128)(2,1)S(1)}, bf16[1,512,2048]{2,1,0:T(8,128)(2,1)}, u32[]{:S(2)}) %copy-start.1) | copy-done | bytes 2097176
  3.2 0.0 copy-start.2
  3.2 0.9 copy-done.2
  4.1 0.0 copy-start.3
  4.1 0.7 copy-done.3
  4.8 0.0 copy-start.4
  4.8 0.7 copy-done.4
  5.5 0.0 copy-start.5
  5.5 0.7 copy-done.5
  6.1 104.4 %moe.1 = bf16[256,256]{1,0:T(8,128)(2,1)S(1)} custom-call(bf16[256,256]{1,0:T(8,128)(2,1)S(1)} %copy-done.2, s32[2,256]{1,0:T(2,128)S(1)} %bitcast.3, s32[2,256]{1,0:T(2,128)S(1)} %bitcast.4, f32[2,256]{1,0:T(2,128)S(1)} %bitcast.5, bf16[1,2048,512]{2,1,0:T(8,128)(2,1)S(1)} %copy-done, bf16[1,512,2048]{2,1,0:T(8,128)(2,1)S(1)} %copy-done.1), custom_call_target="tpu_custom_call" | custom-call | tf_op jit(solution)/shard_map/moe/pallas_call | solution.py:261
  110.6 0.7 copy.8
Async XLA Ops:
  0.0 1.6 %copy-start = (bf16[1,2048,512]{2,1,0:T(8,128)(2,1)S(1)}, bf16[1,2048,512]{2,1,0:T(8,128)(2,1)}, u32[]{:S(2)}) copy-start(bf16[1,2048,512]{2,1,0:T(8,128)(2,1)} %w_in.1) | copy-start | bytes 6291460
  1.6 1.6 %copy-start.1 = (bf16[1,512,2048]{2,1,0:T(8,128)(2,1)S(1)}, bf16[1,512,2048]{2,1,0:T(8,128)(2,1)}, u32[]{:S(2)}) copy-start(bf16[1,512,2048]{2,1,0:T(8,128)(2,1)} %w_out.1) | copy-start | bytes 6291460
  3.2 0.9 copy-start.2
  4.1 0.7 copy-start.3
  4.8 0.7 copy-start.4
  5.5 0.7 copy-start.5

commit v2 on v1

v2 whole, which is shorter than its diff:
```python
import functools

import jax
import jax.numpy as jnp
from jax import lax
from jax.experimental import pallas as pl
from jax.experimental.pallas import tpu as pltpu
from jax.sharding import PartitionSpec as P

MESH = pl.DeviceIdType.MESH
BF, F32 = jnp.bfloat16, jnp.float32

NZ = 16
SUB = 4
CAP = 10
PEERS = 8
UNIT = SUB * CAP
DZ = (1, 2, -1, -2, 3, 4, -3, -4, 5, 6, -5, -6, 0, 7, 8, -7)
SLOT_OF = {d % NZ: k for k, d in enumerate(DZ)}
BACK = tuple(SLOT_OF[(-d) % NZ] for d in DZ)
HALF = NZ * CAP // 2
GROUPS = 4
PER = NZ // GROUPS
ROW = 4
FIRST = {"own": 0, "row": 5, "col": 9, "px": 13, "py": 17, "qx": 21, "qy": 25}


def plan(period, hop, start, wave):
    at = [(-9, "m", 0), (-8, "z", 0), (-7, "m", 1), (-6, "z", 1),
          (wave, "z", 2), (2 * wave, "z", 3), (2 * wave + 0.1, "u", 0), (2 * wave + 0.2, "w", 0)]
    for g in range(GROUPS):
        t = g * period * PER
        at += [(max(t, g * start * PER), "a", g), (t + hop, "b", g), (t + 2 * hop, "d", g),
               (t + 3 * hop, "e", g), (t + 4 * hop, "g", g)]
        if g == GROUPS // 2 - 1:
            at += [(t + 5.5 * hop, "k", 0), (t + 7 * hop, "c", 0)]
    at = sorted(at)
    tail = [("x", i) for i in range(4)] + [("k", 1), ("c", 1)]
    done = [(s, i) for _, s, i in at if (s, i) != ("c", 0)]
    return done + [("c", 0)] + tail


ORDER = plan(1.0, 3.0, 1.0, 0.5)


def places():
    e, t = lax.axis_index("expert"), lax.axis_index("tensor")
    return e // 4, (e // 2) % 2, e % 2, t // 4, t % 4


def kernel(tok_in, ids_in, slot_in, gate_in, w_in, w_out, out,
           tok, ids, slot, gate, in_sem, w1, w2, mix, unmix, gates_hi, gates_lo,
           near_out, near_in, far_out, far_in, part_out, by_x, by_y, last_x, last_y,
           back_out, back_in, last_out, last_in,
           w_sem, near_s, near_r, far_s, far_r, tree_s, tree_r,
           back_s, back_r, last_s, last_r):
    z, ylo, core, yhi, x = places()
    tens = yhi * 4 + x

    def at_sub(i):
        return (z * 4 + ((ylo + i // 2) % 2) * 2 + (core + i % 2) % 2, tens)

    def at_z(d):
        return (((z + d + NZ) % NZ) * 4 + ylo * 2 + core, tens)

    def peer_index(r):
        return ((yhi + r // ROW) % 2) * 4 + (x + r % ROW) % 4

    def at_peer(r):
        return (z * 4 + ylo * 2 + core, peer_index(r))

    def remote(src, dst, s, r, to):
        return pltpu.make_async_remote_copy(
            src_ref=src, dst_ref=dst, send_sem=s, recv_sem=r,
            device_id=to, device_id_type=MESH)

    barrier = pltpu.get_barrier_semaphore()
    partners = ([at_sub(i) for i in range(1, SUB)] + [at_z(d) for d in range(1, NZ)]
                + [at_peer(r) for r in (1, 2, 3, ROW)])
    for p in partners:
        pl.semaphore_signal(barrier, inc=1, device_id=p, device_id_type=MESH)

    firsts = [pltpu.make_async_copy(a, b, in_sem.at[i]) for i, (a, b) in enumerate(
        ((ids_in, ids), (slot_in, slot), (tok_in, tok), (gate_in, gate)))]
    for cp in firsts:
        cp.start()
    loads = []
    for r in range(PEERS):
        j = peer_index(r)
        for h in range(2):
            loads.append(pltpu.make_async_copy(
                w_in.at[0, pl.ds(pl.multiple_of(j * 256 + h * 128, 128), 128), :],
                w1.at[h, pl.ds(r * 128, 128), :], w_sem.at[len(loads)]))
        loads.append(pltpu.make_async_copy(
            w_out.at[0, :, pl.ds(pl.multiple_of(j * 256, 256), 256)],
            w2.at[r], w_sem.at[len(loads)]))
    for c in loads:
        c.start()

    for cp in firsts:
        cp.wait()
    e = ids[...]
    dz = (e // 4 - z + NZ) % NZ
    k = jnp.zeros_like(e)
    for d, s in SLOT_OF.items():
        k = jnp.where(dz == d, s, k)
    sub = ((e // 2 % 2 + ylo) % 2) * 2 + (e % 2 + core) % 2
    c = slot[...]
    half_k = k // (NZ // 2)
    target = jnp.where(c >= 0, (half_k * SUB + sub - half_k) * HALF + k * CAP + c, -1)
    rows = lax.broadcasted_iota(jnp.int32, (SUB * NZ * CAP, 256), 0)
    chosen = (rows == target[0:1, :]) | (rows == target[1:2, :])
    panel = jnp.dot(chosen.astype(F32).astype(BF), tok[...], preferred_element_type=F32)
    near_out[...] = panel.astype(BF).reshape(2, SUB, HALF, 256)

    pl.semaphore_wait(barrier, len(partners))

    near = []
    for half in range(2):
        for i in range(1, SUB):
            cp = remote(near_out.at[half, i], near_in.at[half, i], near_s.at[half, i],
                        near_r.at[half, i], at_sub(i))
            cp.start()
            near.append(cp)
    near_in[:, 0] = near_out[:, 0]

    def near_of_far(i, swap):
        kk = (i * 1639) >> 16
        rest = i - kk * 40
        if swap:
            kk = kk + 1 - 2 * (kk % 2)
        ss = (rest * 205) >> 11
        return ss * HALF + kk * CAP + rest - ss * 10

    n = SUB * HALF
    near_cols = lax.broadcasted_iota(jnp.int32, (n, n), 1)
    near_rows = lax.broadcasted_iota(jnp.int32, (n, n), 0)
    far_rows = lax.broadcasted_iota(jnp.int32, (n, 1), 0)
    far_cols = lax.broadcasted_iota(jnp.int32, (1, n), 1)
    for h in range(2):
        mix[h] = (near_of_far(far_rows, h) == near_cols).astype(F32).astype(BF)

    upper = lax.broadcasted_iota(jnp.int32, (2 * UNIT, 128), 0) < UNIT

    def pick(a, b):
        return jnp.where(upper, a, b)

    far = {}

    def arrange(half):
        for cp in near[half * 3:half * 3 + 3]:
            cp.wait_recv()
        arrived = near_in[half].reshape(n, 256)
        order0 = jnp.dot(mix[0], arrived[:, :128], preferred_element_type=F32)
        order1 = jnp.dot(mix[1], arrived[:, 128:], preferred_element_type=F32)
        for k in range(NZ // 2):
            s = half * (NZ // 2) + k
            a = order0[(k // 2) * 80:(k // 2 + 1) * 80]
            b = order1[(k // 2) * 80:(k // 2 + 1) * 80]
            block = (pick(a, b) if s % 2 == 0 else pick(b, a)).astype(BF)
            if DZ[s] == 0:
                far_in[0, s] = block
            else:
                far_out[s] = block

    def spread(g):
        for s in range(g * 4, g * 4 + 4):
            if DZ[s]:
                far[s] = remote(far_out.at[s], far_in.at[0, BACK[s]], far_s.at[s],
                                far_r.at[BACK[s]], at_z(DZ[s]))
                far[s].start()

    def drain(g):
        for s in range(g * 4, g * 4 + 4):
            if DZ[s]:
                far[s].wait_send()

    def prepare(_):
        for h in range(2):
            unmix[h] = (near_of_far(far_cols, h) == near_rows).astype(F32).astype(BF)
        g = gate[...]
        weighted = jnp.where(rows == target[0:1, :], g[0:1, :], 0.0) + jnp.where(
            rows == target[1:2, :], g[1:2, :], 0.0)
        hi = weighted.astype(BF)
        lo = weighted - hi.astype(F32)
        for half in range(2):
            gates_hi[half] = hi[half * n:(half + 1) * n].astype(F32).T.astype(BF)
            gates_lo[half] = lo[half * n:(half + 1) * n].T.astype(BF)

    def loaded(_):
        for cp in loads:
            cp.wait()

    sent = {}
    backs = []
    H = PER // 2

    def send(g, kind, i, src, dst, to):
        n = FIRST[kind] + i
        cp = remote(src, dst, tree_s.at[g, n], tree_r.at[g, n], at_peer(to))
        cp.start()
        sent[g, kind, i] = cp

    def got(g, kind, *which):
        for i in which:
            sent[g, kind, i].wait_recv()

    def part(g, half):
        return pl.ds(g * PER + half * H, H)

    def gather0(g):
        for s in range(g * PER, (g + 1) * PER):
            if DZ[s]:
                remote(far_out.at[s], far_in.at[0, s], far_s.at[s], far_r.at[s], at_z(DZ[s])).wait_recv()
        whole = pl.ds(g * PER, PER)
        for r in (ROW, 1, 3, 2):
            back = r if r == ROW else 4 - r
            send(g, "own", back, far_in.at[0, whole], far_in.at[back, whole], r)

    def gather1(g):
        got(g, "own", ROW)
        for r in (1, 3, 2):
            send(g, "row", 4 - r, far_in.at[ROW, part(g, 0)], far_in.at[ROW + 4 - r, part(g, 0)], r)
        for r in (1, 3, 2):
            got(g, "own", r)
            send(g, "col", r, far_in.at[r, part(g, 1)], far_in.at[ROW + r, part(g, 1)], ROW)

    def compute(g):
        got(g, "row", 1, 2, 3)
        got(g, "col", 1, 2, 3)
        left0, left1 = [], []
        for q in range(H):
            s = g * PER + 2 * q
            a0 = [far_in[r, s] for r in range(PEERS)]
            a1 = [far_in[r, s + 1] for r in range(PEERS)]
            left0.append(jnp.concatenate([pick(u, v) for u, v in zip(a0, a1)], axis=1))
            left1.append(jnp.concatenate([pick(v, u) for u, v in zip(a0, a1)], axis=1))
        acc0 = jnp.dot(jnp.concatenate(left0, axis=0), w1[0], preferred_element_type=F32)
        acc1 = jnp.dot(jnp.concatenate(left1, axis=0), w1[1], preferred_element_type=F32)
        swapped = []
        for q in range(H):
            swapped += [acc1[q * 80 + 40:q * 80 + 80], acc1[q * 80:q * 80 + 40]]
        v = acc0 + jnp.concatenate(swapped, axis=0)
        inner = 0.7978845608028654 * (v + 0.044715 * (v * v * v))
        hidden = (0.5 * v * (1.0 + jnp.tanh(inner))).astype(BF)
        for r in (5, 1, 7, 3, 6, 2, 4, 0):
            res = jnp.dot(hidden, w2[r], preferred_element_type=F32)
            for q in range(H):
                p0 = res[q * 80:q * 80 + 80, :128]
                p1 = res[q * 80:q * 80 + 80, 128:]
                p1 = jnp.concatenate([p1[40:], p1[:40]], axis=0)
                s = g * PER + 2 * q
                part_out[r // 4, r % 4, s] = pick(p0, p1).astype(BF)
                part_out[r // 4, r % 4, s + 1] = pick(p1, p0).astype(BF)
            if r in (1, 2, 3):
                send(g, "px", 4 - r, part_out.at[:, r, part(g, 0)], by_x.at[g, 4 - r], r)
            if r >= ROW:
                send(g, "py", r - ROW, part_out.at[1, r - ROW, part(g, 1)], by_y.at[g, r - ROW], ROW)

    def scatter1(g):
        for r in (1, 3, 2):
            got(g, "py", r)
            for i in range(H):
                s = g * PER + H + i
                part_out[0, r, s] = (part_out[0, r, s].astype(F32) + by_y[g, r, i].astype(F32)).astype(BF)
            send(g, "qx", 4 - r, part_out.at[0, r, part(g, 1)], last_x.at[g, 4 - r], r)
        got(g, "px", 1, 2, 3)
        for i in range(H):
            s = g * PER + i
            total = part_out[1, 0, s].astype(F32)
            for r in (1, 2, 3):
                total = total + by_x[g, r, 1, i].astype(F32)
            part_out[1, 0, s] = total.astype(BF)
        send(g, "qy", 0, part_out.at[1, 0, part(g, 0)], last_y.at[g], ROW)

    def give_back(s, value):
        if DZ[s] == 0:
            back_in[s] = value.astype(BF)
            return
        back_out[s] = value.astype(BF)
        cp = remote(back_out.at[s], back_in.at[BACK[s]], back_s.at[s], back_r.at[BACK[s]],
                    at_z(DZ[s]))
        cp.start()
        backs.append(cp)

    def finish(g):
        got(g, "qy", 0)
        for i in range(H):
            s = g * PER + i
            total = part_out[0, 0, s].astype(F32) + last_y[g, i].astype(F32)
            for r in (1, 2, 3):
                total = total + by_x[g, r, 0, i].astype(F32)
            give_back(s, total)
        got(g, "py", 0)
        got(g, "qx", 1, 2, 3)
        for i in range(H):
            s = g * PER + H + i
            total = part_out[0, 0, s].astype(F32) + by_y[g, 0, i].astype(F32)
            for r in (1, 2, 3):
                total = total + last_x[g, r, i].astype(F32)
            give_back(s, total)

    last = []

    def returned(half):
        for s in range(half * NZ // 2, (half + 1) * NZ // 2):
            if DZ[s]:
                remote(back_out.at[s], back_in.at[s], back_s.at[s], back_r.at[s],
                       at_z(DZ[s])).wait_recv()
        left0, left1 = [], []
        for q in range(half * NZ // 4, (half + 1) * NZ // 4):
            a, b = back_in[2 * q], back_in[2 * q + 1]
            left0.append(pick(a, b))
            left1.append(pick(b, a))
        res0 = jnp.dot(unmix[0], jnp.concatenate(left0, axis=0), preferred_element_type=F32)
        res1 = jnp.dot(unmix[1], jnp.concatenate(left1, axis=0), preferred_element_type=F32)
        res = jnp.concatenate([res0, res1], axis=1).astype(BF)
        last_in[half, 0] = res[:HALF]
        for i in range(1, SUB):
            last_out[half, i] = res[i * HALF:(i + 1) * HALF]
            cp = remote(last_out.at[half, i], last_in.at[half, i], last_s.at[half, i],
                        last_r.at[half, i], at_sub(i))
            cp.start()
            last.append(cp)

    sums = []

    def combine(half):
        for cp in last[half * 3:half * 3 + 3]:
            cp.wait_recv()
        rows_in = last_in[half].reshape(n, 256)
        sums.append(jnp.dot(gates_hi[half], rows_in, preferred_element_type=F32)
                    + jnp.dot(gates_lo[half], rows_in, preferred_element_type=F32))

    steps = {"m": arrange, "z": spread, "x": drain, "u": prepare, "w": loaded,
             "a": gather0, "b": gather1, "d": compute, "e": scatter1, "g": finish,
             "k": returned, "c": combine}
    for step, i in ORDER:
        steps[step](i)
    out[...] = (sums[0] + sums[1]).astype(BF)
    for cp in near + list(sent.values()) + backs + last:
        cp.wait_send()


def body(tokens, gate_values, expert_ids, slot_index, w_in, w_out):
    n = SUB * NZ * CAP
    vm = pl.BlockSpec(memory_space=pltpu.VMEM)
    hbm = pl.BlockSpec(memory_space=pl.ANY)
    dma = pltpu.SemaphoreType.DMA
    blocks = (NZ, 2 * UNIT, 128)
    return pl.pallas_call(
        kernel,
        out_shape=jax.ShapeDtypeStruct((256, 256), BF),
        in_specs=[hbm] * 6,
        out_specs=vm,
        scratch_shapes=[
            pltpu.VMEM((256, 256), BF), pltpu.VMEM((2, 256), jnp.int32),
            pltpu.VMEM((2, 256), jnp.int32), pltpu.VMEM((2, 256), F32), dma((4,)),
            pltpu.VMEM((2, 1024, 512), BF), pltpu.VMEM((PEERS, 512, 256), BF),
            pltpu.VMEM((2, n // 2, n // 2), BF), pltpu.VMEM((2, n // 2, n // 2), BF),
            pltpu.VMEM((2, 256, n // 2), BF), pltpu.VMEM((2, 256, n // 2), BF),
            pltpu.VMEM((2, SUB, HALF, 256), BF), pltpu.VMEM((2, SUB, HALF, 256), BF),
            pltpu.VMEM(blocks, BF), pltpu.VMEM((PEERS,) + blocks, BF),
            pltpu.VMEM((2, 4) + blocks, BF),
            pltpu.VMEM((GROUPS, 4, 2, PER // 2) + blocks[1:], BF),
            pltpu.VMEM((GROUPS, 4, PER // 2) + blocks[1:], BF),
            pltpu.VMEM((GROUPS, 4, PER // 2) + blocks[1:], BF),
            pltpu.VMEM((GROUPS, PER // 2) + blocks[1:], BF),
            pltpu.VMEM(blocks, BF), pltpu.VMEM(blocks, BF),
            pltpu.VMEM((2, SUB, HALF, 256), BF), pltpu.VMEM((2, SUB, HALF, 256), BF),
            dma((3 * PEERS,)), dma((2, SUB)), dma((2, SUB)), dma((NZ,)), dma((NZ,)),
            dma((GROUPS, 26)), dma((GROUPS, 26)),
            dma((NZ,)), dma((NZ,)), dma((2, SUB)), dma((2, SUB)),
        ],
        compiler_params=pltpu.CompilerParams(
            collective_id=0, has_side_effects=True, vmem_limit_bytes=60 * 2**20),
        name="moe",
    )(tokens, expert_ids.T, slot_index.T, gate_values.T, w_in, w_out)


def solution(mesh):
    placed = (
        P("expert", "tensor"),
        P("expert", None),
        P("expert", None),
        P("expert", None),
        P("expert", None, "tensor"),
        P("expert", "tensor", None),
    )
    return jax.shard_map(
        body, mesh=mesh, in_specs=placed, out_specs=P("expert", "tensor"), check_vma=False
    )
```

time: 113 us -> 90.9 us (0.80); the launches traced: 111 us -> 90.7 us
  Pallas kernels: 104 us -> 89.1 us
  local copies, waits for them, and re-layouts: 6.79 us -> 1.57 us
    pallas_call x1, Pallas kernels: 104 us -> 89.1 us  [body(): pl.pallas_call(kernel, out_shape=jax.ShapeDtypeStruct((256, 256), BF), in...]
    unnamed x13 -> x1, local copies, waits for them, and re-layouts: 6.79 us -> 1.57 us
where the time goes in v2:
time: 90.9 us; the launch traced here: 90.7 us
  Pallas kernels  89.1 us (98%)
  local copies, waits for them, and re-layouts  1.57 us (2%)
    pallas_call x1, Pallas kernels, body(): pl.pallas_call(kernel, out_shape=jax.ShapeDtypeStruct((256, 256), BF), in...  89.1 us

profile of v2, /device:TPU:1, one launch (start us, length us, event | category | flops | bytes accessed | tf_op | source)
XLA Modules:
  0.0 90.7 jit_solution(4677645374157615642)
XLA Ops:
  0.0 89.1 %moe.1 = bf16[256,256]{1,0:T(8,128)(2,1)} custom-call(bf16[256,256]{1,0:T(8,128)(2,1)} %tok_in.1, s32[2,256]{1,0:T(2,128)} %bitcast.3, s32[2,256]{1,0:T(2,128)} %bitcast.4, f32[2,256]{1,0:T(2,128)} %bitcast.5, bf16[1,2048,512]{2,1,0:T(8,128)(2,1)} %w_in.1, bf16[1,512,2048]{2,1,0:T(8,128)(2,1)} %w_out.1), custom_call_target="tpu_custom_call" | custom-call | tf_op jit(solution)/shard_map/moe/pallas_call | solution.py:351
  89.1 1.6 %copy.8 = bf16[256,256]{1,0:T(8,128)(2,1)} copy(bf16[256,256]{1,0:T(8,128)(2,1)} %moe.1) | data formatting | bytes 262144

commit v3 on v2

--- a/solution.py
+++ b/solution.py
@@ -15,7 +15,7 @@
 CAP = 10
 PEERS = 8
 UNIT = SUB * CAP
-DZ = (1, 2, -1, -2, 3, 4, -3, -4, 5, 6, -5, -6, 0, 7, 8, -7)
+DZ = (1, 2, -1, -2, 3, 4, -3, -4, 0, 7, 8, -7, 5, 6, -5, -6)
 SLOT_OF = {d % NZ: k for k, d in enumerate(DZ)}
 BACK = tuple(SLOT_OF[(-d) % NZ] for d in DZ)
 HALF = NZ * CAP // 2
@@ -243,7 +243,7 @@
         v = acc0 + jnp.concatenate(swapped, axis=0)
         inner = 0.7978845608028654 * (v + 0.044715 * (v * v * v))
         hidden = (0.5 * v * (1.0 + jnp.tanh(inner))).astype(BF)
-        for r in (5, 1, 7, 3, 6, 2, 4, 0):
+        for r in (5, 7, 6, 1, 3, 2, 4, 0):
             res = jnp.dot(hidden, w2[r], preferred_element_type=F32)
             for q in range(H):
                 p0 = res[q * 80:q * 80 + 80, :128]

time: 90.9 us -> 89.8 us (0.988)
  Pallas kernels: 89.1 us -> 88.1 us
    pallas_call x1, Pallas kernels: 89.1 us -> 88.1 us  [body(): pl.pallas_call(kernel, out_shape=jax.ShapeDtypeStruct((256, 256), BF), in...]
where the time goes in v3:
time: 89.8 us; the launch traced here: 89.7 us
  Pallas kernels  88.1 us (98%)
  local copies, waits for them, and re-layouts  1.57 us (2%)
    pallas_call x1, Pallas kernels, body(): pl.pallas_call(kernel, out_shape=jax.ShapeDtypeStruct((256, 256), BF), in...  88.1 us

profile of v3, /device:TPU:1, one launch (start us, length us, event | category | flops | bytes accessed | tf_op | source)
XLA Modules:
  0.0 89.7 jit_solution(330904029761939339)
XLA Ops:
  0.0 88.1 %moe.1 = bf16[256,256]{1,0:T(8,128)(2,1)} custom-call(bf16[256,256]{1,0:T(8,128)(2,1)} %tok_in.1, s32[2,256]{1,0:T(2,128)} %bitcast.3, s32[2,256]{1,0:T(2,128)} %bitcast.4, f32[2,256]{1,0:T(2,128)} %bitcast.5, bf16[1,2048,512]{2,1,0:T(8,128)(2,1)} %w_in.1, bf16[1,512,2048]{2,1,0:T(8,128)(2,1)} %w_out.1), custom_call_target="tpu_custom_call" | custom-call | tf_op jit(solution)/shard_map/moe/pallas_call | solution.py:351
  88.1 1.6 %copy.8 = bf16[256,256]{1,0:T(8,128)(2,1)} copy(bf16[256,256]{1,0:T(8,128)(2,1)} %moe.1) | data formatting | bytes 262144

commit v4 on v3

--- a/solution.py
+++ b/solution.py
@@ -22,7 +22,7 @@
 GROUPS = 4
 PER = NZ // GROUPS
 ROW = 4
-FIRST = {"own": 0, "row": 5, "col": 9, "px": 13, "py": 17, "qx": 21, "qy": 25}
+FIRST = {"own": 0, "row": 5, "col": 9, "px": 13, "py": 17, "qx": 21, "qy": 25, "rest": 26}
 
 
 def plan(period, hop, start, wave):
@@ -33,7 +33,7 @@
         at += [(max(t, g * start * PER), "a", g), (t + hop, "b", g), (t + 2 * hop, "d", g),
                (t + 3 * hop, "e", g), (t + 4 * hop, "g", g)]
         if g == GROUPS // 2 - 1:
-            at += [(t + 5.5 * hop, "k", 0), (t + 7 * hop, "c", 0)]
+            at += [(t + 6 * hop, "k", 0), (t + 7 * hop, "c", 0)]
     at = sorted(at)
     tail = [("x", i) for i in range(4)] + [("k", 1), ("c", 1)]
     done = [(s, i) for _, s, i in at if (s, i) != ("c", 0)]
@@ -212,10 +212,11 @@
         for s in range(g * PER, (g + 1) * PER):
             if DZ[s]:
                 remote(far_out.at[s], far_in.at[0, s], far_s.at[s], far_r.at[s], at_z(DZ[s])).wait_recv()
-        whole = pl.ds(g * PER, PER)
-        for r in (ROW, 1, 3, 2):
-            back = r if r == ROW else 4 - r
-            send(g, "own", back, far_in.at[0, whole], far_in.at[back, whole], r)
+        for kind in ("own", "rest"):
+            for r in (ROW, 1, 3, 2):
+                back = r if r == ROW else 4 - r
+                piece = part(g, int((r == ROW) == (kind == "rest")))
+                send(g, kind, back, far_in.at[0, piece], far_in.at[back, piece], r)
 
     def gather1(g):
         got(g, "own", ROW)
@@ -226,6 +227,7 @@
             send(g, "col", r, far_in.at[r, part(g, 1)], far_in.at[ROW + r, part(g, 1)], ROW)
 
     def compute(g):
+        got(g, "rest", 1, 2, 3, ROW)
         got(g, "row", 1, 2, 3)
         got(g, "col", 1, 2, 3)
         left0, left1 = [], []
@@ -369,7 +371,7 @@
             pltpu.VMEM(blocks, BF), pltpu.VMEM(blocks, BF),
             pltpu.VMEM((2, SUB, HALF, 256), BF), pltpu.VMEM((2, SUB, HALF, 256), BF),
             dma((3 * PEERS,)), dma((2, SUB)), dma((2, SUB)), dma((NZ,)), dma((NZ,)),
-            dma((GROUPS, 26)), dma((GROUPS, 26)),
+            dma((GROUPS, 31)), dma((GROUPS, 31)),
             dma((NZ,)), dma((NZ,)), dma((2, SUB)), dma((2, SUB)),
         ],
         compiler_params=pltpu.CompilerParams(

time: 89.8 us -> 89.9 us (level)
  no operation moved by 1% of the time
where the time goes in v4:
time: 89.9 us; the launch traced here: 89.2 us
  Pallas kernels  87.7 us (98%)
  local copies, waits for them, and re-layouts  1.57 us (2%)
    pallas_call x1, Pallas kernels, body(): pl.pallas_call(kernel, out_shape=jax.ShapeDtypeStruct((256, 256), BF), in...  87.7 us

profile of v4, /device:TPU:1, one launch (start us, length us, event | category | flops | bytes accessed | tf_op | source)
XLA Modules:
  0.0 89.2 jit_solution(16190656217152850045)
XLA Ops:
  0.0 87.7 %moe.1 = bf16[256,256]{1,0:T(8,128)(2,1)} custom-call(bf16[256,256]{1,0:T(8,128)(2,1)} %tok_in.1, s32[2,256]{1,0:T(2,128)} %bitcast.3, s32[2,256]{1,0:T(2,128)} %bitcast.4, f32[2,256]{1,0:T(2,128)} %bitcast.5, bf16[1,2048,512]{2,1,0:T(8,128)(2,1)} %w_in.1, bf16[1,512,2048]{2,1,0:T(8,128)(2,1)} %w_out.1), custom_call_target="tpu_custom_call" | custom-call | tf_op jit(solution)/shard_map/moe/pallas_call | solution.py:353
  87.7 1.6 %copy.8 = bf16[256,256]{1,0:T(8,128)(2,1)} copy(bf16[256,256]{1,0:T(8,128)(2,1)} %moe.1) | data formatting | bytes 262144
